TPU v7x, 32 devices: a whole 2x2x4 slice. The times are simulated.
32 devices in a mesh: ingest: 16 (over z, y, x), codes: 2 (over core).
Axes of the slice: x: 2, y: 2, z: 4, core: 2. Of those that a mesh axis runs over, the one named last changes fastest.
Arguments:
- vectors: bfloat16 [4096, 1024], P('ingest'), may hold values from -6 to 6
- codes: int32 [2, 4096], P(None, 'ingest'), may hold values from 0 to 4095, as said below
- codebook: bfloat16 [2, 4096, 1024], P('codes', 'ingest'), may hold values from -5 to 5
- pairs: int32 [64, 64], replicated, may hold values from 0 to 63, as said below
Outputs:
- new_codebook: float32 [2, 4096, 1024], P('codes', 'ingest')
- gram: float32 [2, 4096, 8192], P('codes', 'ingest')
Inputs may be any that keep to these rules, and one draw needn't show every extreme that they name: In each codebook and each aligned block of 256 vectors (the vectors of one index of ingest), at most 32 codes fall in any one range j * 256 to (j + 1) * 256 - 1; in each codebook one such range holds exactly 32 codes of every block. `pairs`: block s is codes (s % 32) * 128 to (s % 32) * 128 + 127 of codebook s // 32; every entry of row r names a block of a codebook other than that of block r; entries may repeat.
All inputs are finite; a program needn't handle non-finite values.
Results may differ from a plain program's by a relative error of at most 0.015.
Values may be sent and summed in bfloat16 or wider, within the bound.
A program may use at most 64 MiB of HBM per device.

v0:
```python
import jax
import jax.numpy as jnp
from jax import lax
from jax.sharding import PartitionSpec as P

K = 4096
BLK = 128
P_SIZE = 64
KB = 32


def shards(vectors, codes, codebook, pairs):
    owners = lax.axis_size("ingest")
    my_owner = lax.axis_index("ingest")
    my_group = lax.axis_index("codes")
    rows_count = vectors.shape[0]
    books_dev = codebook.shape[0]
    own_rows = codebook.shape[1]
    feature_dim = codebook.shape[2]
    codebooks = codes.shape[0]
    capacity = 2 * rows_count // owners
    slot_total = owners * books_dev * capacity
    local_codes = lax.dynamic_slice_in_dim(codes, my_group * books_dev, books_dev, 0)
    target = local_codes // own_rows
    within = local_codes - target * own_rows
    owner_hits = (target[:, :, None] == jnp.arange(owners, dtype=jnp.int32)).astype(jnp.int32)
    before = jnp.cumsum(owner_hits, axis=1) - owner_hits
    slot_rank = jnp.sum(before * owner_hits, axis=2)
    book_offset = jnp.arange(books_dev, dtype=jnp.int32)[:, None]
    slot_index = (target * books_dev + book_offset) * capacity + slot_rank
    slot_flat = slot_index.reshape(-1)
    vector_ids = jnp.broadcast_to(
        jnp.arange(rows_count, dtype=jnp.int32), (books_dev, rows_count)
    ).reshape(-1)
    slot_vector = jnp.full((slot_total,), rows_count, jnp.int32).at[slot_flat].set(vector_ids)
    asked_rows = (within + book_offset * own_rows).reshape(-1)
    slot_request = jnp.full((slot_total,), -1, jnp.int32).at[slot_flat].set(asked_rows)
    slot_request = slot_request.reshape(owners, books_dev * capacity)
    flat_book = codebook.reshape(books_dev * own_rows, feature_dim)
    picked = jnp.take(
        flat_book,
        jnp.maximum(
            lax.all_to_all(slot_request, "ingest", split_axis=0, concat_axis=0, tiled=True), 0
        ),
        axis=0,
    )
    returned = lax.all_to_all(picked, "ingest", split_axis=0, concat_axis=0, tiled=True)
    fetched = jnp.take(returned.reshape(slot_total, feature_dim), slot_index, axis=0)
    partial_sum = jnp.sum(fetched.astype(jnp.float32), axis=0)
    full_sum = lax.psum(partial_sum.astype(jnp.bfloat16), "codes").astype(jnp.float32)
    residual = (vectors.astype(jnp.float32) - full_sum).astype(jnp.bfloat16)
    residual_ext = jnp.concatenate([residual, jnp.zeros((1, feature_dim), jnp.bfloat16)], axis=0)
    codes_ext = jnp.concatenate([codes.T, jnp.full((1, codebooks), -1, jnp.int32)], axis=0)
    send_rows = jnp.take(residual_ext, slot_vector, axis=0).reshape(
        owners, books_dev * capacity, feature_dim
    )
    send_codes = jnp.take(codes_ext, slot_vector, axis=0).reshape(
        owners, books_dev * capacity, codebooks
    )
    got_rows, got_codes = (
        lax.all_to_all(send_rows, "ingest", split_axis=0, concat_axis=0, tiled=True),
        lax.all_to_all(send_codes, "ingest", split_axis=0, concat_axis=0, tiled=True),
    )
    got_rows = got_rows.reshape(owners, books_dev, capacity, feature_dim)
    got_codes = got_codes.reshape(owners, books_dev, capacity, codebooks)
    block_rows = min(own_rows, BLK)
    pieces = own_rows // block_rows
    group_size = min(P_SIZE, 8)
    contract = (((0,), (0,)), ((), ()))
    rows_in = got_rows[:, 0].reshape(owners * capacity, feature_dim)
    tuples = got_codes[:, 0].reshape(owners * capacity, codebooks)
    book_global = my_group * books_dev + 0
    own_code = lax.dynamic_index_in_dim(tuples, book_global, 1, keepdims=False)
    local_row = own_code - my_owner * own_rows
    member = (local_row[:, None] == jnp.arange(own_rows, dtype=jnp.int32)).astype(jnp.bfloat16)
    right_side = lax.dot_general(member, rows_in, contract, preferred_element_type=jnp.float32)
    code_count = jnp.sum(member, axis=0, dtype=jnp.float32)
    current = codebook[0].astype(jnp.float32)
    updated_list = [current + (right_side - 2.0 * current) / (code_count[:, None] + 2.0)]
    gram_pieces = []
    for part_index in range(pieces):
        first_row = book_global * K + my_owner * own_rows + part_index * block_rows
        partner = lax.dynamic_index_in_dim(pairs, first_row // BLK, 0, keepdims=False)
        partner_book = partner // KB
        partner_start = partner % KB * BLK
        partner_code = jnp.take(tuples, partner_book, axis=1) - partner_start[None, :]
        member_part = member[:, part_index * block_rows : (part_index + 1) * block_rows]
        columns = []
        for group_index in range(P_SIZE // group_size):
            chosen = partner_code[:, group_index * group_size : (group_index + 1) * group_size]
            onehot_table = (chosen[:, :, None] == jnp.arange(BLK, dtype=jnp.int32)).astype(
                jnp.bfloat16
            )
            onehot_table = onehot_table.reshape(chosen.shape[0], group_size * BLK)
            columns.append(
                lax.dot_general(
                    member_part, onehot_table, contract, preferred_element_type=jnp.float32
                )
            )
        gram_pieces.append(jnp.concatenate(columns, axis=1))
    gram_list = [jnp.concatenate(gram_pieces, axis=0)]
    return (jnp.stack(updated_list), jnp.stack(gram_list))


def solution(mesh):
    in_specs = (P("ingest", None), P(None, "ingest"), P("codes", "ingest", None), P())
    out_specs = (P("codes", "ingest", None), P("codes", "ingest", None))
    return jax.shard_map(shards, mesh=mesh, in_specs=in_specs, out_specs=out_specs, check_vma=False)
```

profile of v0, /device:TPU:0, one launch (start us, length us, event | category | flops | bytes accessed | tf_op | source)
XLA Modules:
  0.0 146.5 jit_solution(7996267810329686315)
XLA Ops:
  11.1 8.3 %all-to-all-start.1 = ((s32[16,1,32]{2,1,0:T(1,128)}), s32[16,1,32]{2,1,0:T(1,128)S(1)}, u32[]{:S(2)}, u32[]{:S(2)}) async-start(s32[16,1,32]{2,1,0:T(1,128)} %all_to_all.16), calls=%async_computation.1 | async-start | bytes 16384 | tf_op jit(solution)/shard_map/all_to_all | solution.py:43
  26.6 6.7 %all-to-all-start = ((s32[16,32,2]{1,2,0:T(2,128)}), s32[16,32,2]{1,2,0:T(2,128)S(1)}, u32[]{:S(2)}, u32[]{:S(2)}) async-start(s32[16,32,2]{1,2,0:T(2,128)} %broadcast_select_fusion.3), calls=%async_computation | async-start | bytes 32768 | tf_op jit(solution)/shard_map/all_to_all | solution.py:62
  33.4 2.1 %gather_fusion.1 = bf16[512,1024]{1,0:T(8,128)(2,1)S(1)} fusion(bf16[256,1024]{1,0:T(8,128)(2,1)S(1)} %bitcast.170, s32[1024]{0:T(1024)S(1)} %pad_clamp_fusion.3), kind=kCustom, calls=%fused_computation.3 | custom fusion | bytes 2099200 | tf_op jit(solution)/shard_map/jit(_take)/gather | solution.py:40
  36.6 4.0 %all-to-all-done = s32[16,32,2]{1,2,0:T(2,128)S(1)} async-done(((s32[16,32,2]{1,2,0:T(2,128)}), s32[16,32,2]{1,2,0:T(2,128)S(1)}, u32[]{:S(2)}, u32[]{:S(2)}) %all-to-all-start) | async-done | bytes 4128 | tf_op jit(solution)/shard_map/all_to_all | solution.py:62
  40.6 3.7 %all-to-all-start.2 = ((bf16[16,32,1024]{2,1,0:T(8,128)(2,1)}), bf16[16,32,1024]{2,1,0:T(8,128)(2,1)S(1)}, u32[]{:S(2)}, u32[]{:S(2)}) async-start(bf16[16,32,1024]{2,1,0:T(8,128)(2,1)} %broadcast_select_fusion), calls=%async_computation.2 | async-start | bytes 2097152 | tf_op jit(solution)/shard_map/all_to_all | solution.py:47
  50.3 1.6 %eq.370 = s32[512,8,128]{2,1,0:T(8,128)S(1)} broadcast(s32[512,8]{1,0:T(8,128)} %copy.97), dimensions={0,1} | broadcast | bytes 2113536 | tf_op jit(solution)/shard_map/eq | solution.py:91
  54.0 1.5 %fusion.26 = f32[128,8192]{1,0:T(8,128)} fusion(s32[64,8,8,128]{3,2,1,0:T(8,128)S(1)} %bitcast.187, s32[1024]{0:T(1024)S(1)} %iota_bitcast_fusion, pred[512,256]{1,0:T(32,128)(4,1)S(1)} %iota_compare_fusion), kind=kOutput, calls=%fused_computation.53 | convolution fusion | flops 134742016 | bytes 2691072 | tf_op jit(solution)/shard_map/dot_general | solution.py:96
  58.7 1.5 %fusion.33 = f32[128,8192]{1,0:T(8,128)} fusion(f32[128,8192]{1,0:T(8,128)} %fusion.34, s32[64,8,8,128]{3,2,1,0:T(8,128)S(1)} %bitcast.173, s32[1024]{0:T(1024)S(1)} %iota_bitcast_fusion, pred[512,256]{1,0:T(32,128)(4,1)S(1)} %iota_compare_fusion), kind=kOutput, calls=%fused_computation.60 | convolution fusion | flops 134742016 | bytes 2691072 | tf_op jit(solution)/shard_map/dot_general | solution.py:96
  60.8 1.5 %fusion.32 = f32[128,8192]{1,0:T(8,128)} fusion(f32[128,8192]{1,0:T(8,128)} %fusion.33, s32[64,8,8,128]{3,2,1,0:T(8,128)S(1)} %bitcast.174, s32[1024]{0:T(1024)S(1)} %iota_bitcast_fusion, pred[512,256]{1,0:T(32,128)(4,1)S(1)} %iota_compare_fusion), kind=kOutput, calls=%fused_computation.59 | convolution fusion | flops 134742016 | bytes 2691072 | tf_op jit(solution)/shard_map/dot_general | solution.py:96
  62.9 1.5 %fusion.31 = f32[128,8192]{1,0:T(8,128)} fusion(f32[128,8192]{1,0:T(8,128)} %fusion.32, s32[64,8,8,128]{3,2,1,0:T(8,128)S(1)} %bitcast.175, s32[1024]{0:T(1024)S(1)} %iota_bitcast_fusion, pred[512,256]{1,0:T(32,128)(4,1)S(1)} %iota_compare_fusion), kind=kOutput, calls=%fused_computation.58 | convolution fusion | flops 134742016 | bytes 2691072 | tf_op jit(solution)/shard_map/dot_general | solution.py:96
  67.1 1.5 %fusion.29 = f32[128,8192]{1,0:T(8,128)} fusion(f32[128,8192]{1,0:T(8,128)} %fusion.30, s32[64,8,8,128]{3,2,1,0:T(8,128)S(1)} %bitcast.177, s32[1024]{0:T(1024)S(1)} %iota_bitcast_fusion, pred[512,256]{1,0:T(32,128)(4,1)S(1)} %iota_compare_fusion), kind=kOutput, calls=%fused_computation.56 | convolution fusion | flops 134742016 | bytes 2691072 | tf_op jit(solution)/shard_map/dot_general | solution.py:96
  73.5 1.6 %fusion.25 = f32[128,8192]{1,0:T(8,128)} fusion(f32[128,8192]{1,0:T(8,128)} %fusion.26, s32[64,8,8,128]{3,2,1,0:T(8,128)S(1)} %bitcast.180, s32[1024]{0:T(1024)S(1)} %iota_bitcast_fusion, pred[512,256]{1,0:T(32,128)(4,1)S(1)} %iota_compare_fusion), kind=kOutput, calls=%fused_computation.52 | convolution fusion | flops 134742016 | bytes 2691072 | tf_op jit(solution)/shard_map/dot_general | solution.py:96
  75.6 1.8 %fusion.24 = f32[128,8192]{1,0:T(8,128)} fusion(f32[128,8192]{1,0:T(8,128)} %fusion.25, s32[64,8,8,128]{3,2,1,0:T(8,128)S(1)} %bitcast.181, s32[1024]{0:T(1024)S(1)} %iota_bitcast_fusion, pred[512,256]{1,0:T(32,128)(4,1)S(1)} %iota_compare_fusion), kind=kOutput, calls=%fused_computation.51 | convolution fusion | flops 134742016 | bytes 2691072 | tf_op jit(solution)/shard_map/dot_general | solution.py:96
  78.0 1.6 %fusion.23 = f32[128,8192]{1,0:T(8,128)} fusion(f32[128,8192]{1,0:T(8,128)} %fusion.24, s32[64,8,8,128]{3,2,1,0:T(8,128)S(1)} %bitcast.182, s32[1024]{0:T(1024)S(1)} %iota_bitcast_fusion, pred[512,256]{1,0:T(32,128)(4,1)S(1)} %iota_compare_fusion), kind=kOutput, calls=%fused_computation.50 | convolution fusion | flops 134742016 | bytes 2691072 | tf_op jit(solution)/shard_map/dot_general | solution.py:96
  83.3 1.6 %fusion.22 = f32[128,8192]{1,0:T(8,128)} fusion(f32[128,8192]{1,0:T(8,128)} %fusion.23, s32[64,8,8,128]{3,2,1,0:T(8,128)S(1)} %bitcast.183, s32[1024]{0:T(1024)S(1)} %iota_bitcast_fusion, pred[512,256]{1,0:T(32,128)(4,1)S(1)} %iota_compare_fusion), kind=kOutput, calls=%fused_computation.49 | convolution fusion | flops 134742016 | bytes 2691072 | tf_op jit(solution)/shard_map/dot_general | solution.py:96
  84.8 17.3 %all-reduce.4.cloned.1.call-done = bf16[256,1024]{1,0:T(8,128)(2,1)} async-done(((bf16[256,1024]{1,0:T(8,128)(2,1)}), bf16[256,1024]{1,0:T(8,128)(2,1)}) %all-reduce.4.cloned.1.call-update) | async-done | bytes 524304 | tf_op jit(solution)/shard_map/psum | solution.py:50
  103.4 2.1 %gather_fusion.3 = bf16[512,1024]{1,0:T(8,128)(2,1)S(1)} fusion(bf16[257,1024]{1,0:T(8,128)(2,1)S(1)} %concatenate.16, s32[1024]{0:T(1024)S(1)} %pad_clamp_fusion.4), kind=kCustom, calls=%fused_computation.5 | custom fusion | bytes 2099200 | tf_op jit(solution)/shard_map/jit(_take)/gather | solution.py:54
  106.6 6.8 %all-to-all-start.3 = ((bf16[16,32,1024]{2,1,0:T(8,128)(2,1)}), bf16[16,32,1024]{2,1,0:T(8,128)(2,1)S(1)}, u32[]{:S(2)}, u32[]{:S(2)}) async-start(bf16[16,32,1024]{2,1,0:T(8,128)(2,1)} %broadcast_select_fusion.1), calls=%async_computation.3 | async-start | bytes 2097152 | tf_op jit(solution)/shard_map/all_to_all | solution.py:61
  114.0 1.5 %fusion.21 = f32[128,8192]{1,0:T(8,128)} fusion(f32[128,8192]{1,0:T(8,128)} %fusion.22, s32[64,8,8,128]{3,2,1,0:T(8,128)S(1)} %bitcast.184, s32[1024]{0:T(1024)S(1)} %iota_bitcast_fusion, pred[512,256]{1,0:T(32,128)(4,1)S(1)} %iota_compare_fusion), kind=kOutput, calls=%fused_computation.48 | convolution fusion | flops 134742016 | bytes 2691072 | tf_op jit(solution)/shard_map/dot_general | solution.py:96
  116.1 1.5 %fusion.20 = f32[128,8192]{1,0:T(8,128)} fusion(f32[128,8192]{1,0:T(8,128)} %fusion.21, s32[64,8,8,128]{3,2,1,0:T(8,128)S(1)} %bitcast.185, s32[1024]{0:T(1024)S(1)} %iota_bitcast_fusion, pred[512,256]{1,0:T(32,128)(4,1)S(1)} %iota_compare_fusion), kind=kOutput, calls=%fused_computation.47 | convolution fusion | flops 134742016 | bytes 2691072 | tf_op jit(solution)/shard_map/dot_general | solution.py:96
  118.3 1.5 %fusion.19 = f32[128,8192]{1,0:T(8,128)} fusion(f32[128,8192]{1,0:T(8,128)} %fusion.20, s32[64,8,8,128]{3,2,1,0:T(8,128)S(1)} %bitcast.172, s32[1024]{0:T(1024)S(1)} %iota_bitcast_fusion, pred[512,256]{1,0:T(32,128)(4,1)S(1)} %iota_compare_fusion), kind=kOutput, calls=%fused_computation.46 | convolution fusion | flops 134742016 | bytes 2691072 | tf_op jit(solution)/shard_map/dot_general | solution.py:96
  119.9 6.9 %maximum_bitcast_fusion = f32[1,256,8192]{2,1,0:T(8,128)} fusion(f32[128,8192]{1,0:T(8,128)} %fusion.19, f32[128,8192]{1,0:T(8,128)S(1)} %copy-done.1), kind=kLoop, calls=%fused_computation.8 | loop fusion | flops 2097152 | bytes 16777216 | tf_op jit(solution)/shard_map/stack | solution.py:102
  126.8 11.3 %all-to-all-done.3 = bf16[16,32,1024]{2,1,0:T(8,128)(2,1)S(1)} async-done(((bf16[16,32,1024]{2,1,0:T(8,128)(2,1)}), bf16[16,32,1024]{2,1,0:T(8,128)(2,1)S(1)}, u32[]{:S(2)}, u32[]{:S(2)}) %all-to-all-start.3) | async-done | bytes 1048608 | tf_op jit(solution)/shard_map/all_to_all | solution.py:61
  138.1 1.6 %fusion.18 = f32[1,256,1024]{2,1,0:T(8,128)} fusion(bf16[512,1024]{1,0:T(8,128)(2,1)S(1)} %bitcast.190, f32[256]{0:T(256)S(1)} %broadcast_add_fusion, s32[512]{0:T(512)S(1)} %bitcast.202, bf16[1,256,1024]{2,1,0:T(8,128)(2,1)S(1)} %copy-done), kind=kOutput, calls=%fused_computation.44 | convolution fusion | flops 269877248 | bytes 2624512 | tf_op jit(solution)/shard_map/dot_general | solution.py:76
  (122 shorter events, 41.2 us)
Async XLA Ops:
  7.2 26.3 %copy-start = (bf16[1,256,1024]{2,1,0:T(8,128)(2,1)S(1)}, bf16[1,256,1024]{2,1,0:T(8,128)(2,1)}, u32[]{:S(2)}) copy-start(bf16[1,256,1024]{2,1,0:T(8,128)(2,1)} %param.8) | copy-start | bytes 1572868
  11.1 15.5 %all-to-all-start.1 = ((s32[16,1,32]{2,1,0:T(1,128)}), s32[16,1,32]{2,1,0:T(1,128)S(1)}, u32[]{:S(2)}, u32[]{:S(2)}) async-start(s32[16,1,32]{2,1,0:T(1,128)} %all_to_all.16), calls=%async_computation.1 | async-start | bytes 16384 | tf_op jit(solution)/shard_map/all_to_all | solution.py:43
  26.6 14.0 %all-to-all-start = ((s32[16,32,2]{1,2,0:T(2,128)}), s32[16,32,2]{1,2,0:T(2,128)S(1)}, u32[]{:S(2)}, u32[]{:S(2)}) async-start(s32[16,32,2]{1,2,0:T(2,128)} %broadcast_select_fusion.3), calls=%async_computation | async-start | bytes 32768 | tf_op jit(solution)/shard_map/all_to_all | solution.py:62
  40.6 38.9 %all-to-all-start.2 = ((bf16[16,32,1024]{2,1,0:T(8,128)(2,1)}), bf16[16,32,1024]{2,1,0:T(8,128)(2,1)S(1)}, u32[]{:S(2)}, u32[]{:S(2)}) async-start(bf16[16,32,1024]{2,1,0:T(8,128)(2,1)} %broadcast_select_fusion), calls=%async_computation.2 | async-start | bytes 2097152 | tf_op jit(solution)/shard_map/all_to_all | solution.py:47
  44.3 57.8 %all-reduce.4.cloned.1.call-start = ((), (), s32[]{:S(2)}) async-start(), calls=%async_computation.4 | async-start | bytes 1048576 | tf_op jit(solution)/shard_map/psum | solution.py:50
  54.0 1.6 %copy-start.13 = (s32[512,8]{0,1:T(8,128)S(1)}, s32[512,8]{0,1:T(8,128)}, u32[]{:S(2)}) copy-start(s32[512,8]{0,1:T(8,128)} %get-tuple-element.25) | copy-start | bytes 49156
  54.0 2.4 %copy-start.12 = (s32[512,8]{0,1:T(8,128)S(1)}, s32[512,8]{0,1:T(8,128)}, u32[]{:S(2)}) copy-start(s32[512,8]{0,1:T(8,128)} %get-tuple-element.24) | copy-start | bytes 49156
  54.0 3.2 %copy-start.11 = (s32[512,8]{0,1:T(8,128)S(1)}, s32[512,8]{0,1:T(8,128)}, u32[]{:S(2)}) copy-start(s32[512,8]{0,1:T(8,128)} %get-tuple-element.23) | copy-start | bytes 49156
  58.1 2.1 %copy-start.2 = (s32[512,8]{1,0:T(8,128)S(1)}, s32[512,8]{1,0:T(8,128)}, u32[]{:S(2)}) copy-start(s32[512,8]{1,0:T(8,128)} %copy.99) | copy-start | bytes 49156
  70.7 2.1 %copy-start.5 = (s32[512,8]{1,0:T(8,128)S(1)}, s32[512,8]{1,0:T(8,128)}, u32[]{:S(2)}) copy-start(s32[512,8]{1,0:T(8,128)} %copy.106) | copy-start | bytes 49156
  72.9 2.2 %copy-start.4 = (s32[512,8]{1,0:T(8,128)S(1)}, s32[512,8]{1,0:T(8,128)}, u32[]{:S(2)}) copy-start(s32[512,8]{1,0:T(8,128)} %copy.107) | copy-start | bytes 49156
  75.0 2.4 %copy-start.3 = (s32[512,8]{1,0:T(8,128)S(1)}, s32[512,8]{1,0:T(8,128)}, u32[]{:S(2)}) copy-start(s32[512,8]{1,0:T(8,128)} %copy.108) | copy-start | bytes 49156
  79.6 1.5 %copy-start.14 = (pred[256]{0:T(512)(128)(4,1)S(1)}, pred[256]{0:T(512)(128)(4,1)}, u32[]{:S(2)}) copy-start(pred[256]{0:T(512)(128)(4,1)} %get-tuple-element.7) | copy-start | bytes 772
  79.6 2.6 %copy-start.10 = (s32[512,8]{0,1:T(8,128)S(1)}, s32[512,8]{0,1:T(8,128)}, u32[]{:S(2)}) copy-start(s32[512,8]{0,1:T(8,128)} %get-tuple-element.22) | copy-start | bytes 49156
  79.6 2.7 %copy-start.9 = (s32[512,8]{0,1:T(8,128)S(1)}, s32[512,8]{0,1:T(8,128)}, u32[]{:S(2)}) copy-start(s32[512,8]{0,1:T(8,128)} %get-tuple-element.21) | copy-start | bytes 49156
  81.0 1.4 copy-start.8
  81.0 1.5 %copy-start.7 = (s32[512,8]{0,1:T(8,128)S(1)}, s32[512,8]{0,1:T(8,128)}, u32[]{:S(2)}) copy-start(s32[512,8]{0,1:T(8,128)} %get-tuple-element.19) | copy-start | bytes 49156
  82.7 19.4 %copy-start.6 = (bf16[256,1024]{1,0:T(8,128)(2,1)S(1)}, bf16[256,1024]{1,0:T(8,128)(2,1)}, u32[]{:S(2)}) copy-start(bf16[256,1024]{1,0:T(8,128)(2,1)} %param.6) | copy-start | bytes 1572868
  106.6 31.5 %all-to-all-start.3 = ((bf16[16,32,1024]{2,1,0:T(8,128)(2,1)}), bf16[16,32,1024]{2,1,0:T(8,128)(2,1)S(1)}, u32[]{:S(2)}, u32[]{:S(2)}) async-start(bf16[16,32,1024]{2,1,0:T(8,128)(2,1)} %broadcast_select_fusion.1), calls=%async_computation.3 | async-start | bytes 2097152 | tf_op jit(solution)/shard_map/all_to_all | solution.py:61
  117.7 2.2 %copy-start.1 = (f32[128,8192]{1,0:T(8,128)S(1)}, f32[128,8192]{1,0:T(8,128)}, u32[]{:S(2)}) copy-start(f32[128,8192]{1,0:T(8,128)} %fusion.27) | copy-start | bytes 12582916
Sparse Core Ops, SparseCore 0:
  82.1 19.9 all-reduce.3
where the time goes:
time: 147 us
  waiting for transfers between devices  32.8 us (22%)
  local copies, waits for them, and re-layouts  30.6 us (21%)
  matrix products  26.3 us (18%)
  starting transfers between devices  25.7 us (17%)
  other arithmetic  16.7 us (11%)
  between operations  14.5 us (10%)
    dot_general x16, matrix products, shards(): lax.dot_general(member_part, onehot_table, contract, preferred_element_ty...  24.7 us
    psum x1, waiting for transfers between devices, shards(): lax.psum(partial_sum.astype(jnp.bfloat16), 'codes').astype(jnp.float32)  17.3 us
    all_to_all x1, waiting for transfers between devices, shards(): lax.all_to_all(send_rows, 'ingest', split_axis=0, concat_axis=0, tiled=True)  11.3 us
    eq x17, local copies, waits for them, and re-layouts, shards(): chosen[:, :, None] == jnp.arange(BLK, dtype=jnp.int32)  10.5 us
    all_to_all x1, starting transfers between devices, shards(): lax.all_to_all(slot_request, 'ingest', split_axis=0, concat_axis=0, tiled...  8.31 us
    slice x18, local copies, waits for them, and re-layouts, shards(): partner_code[:, group_index * group_size:(group_index + 1) * group_size]  6.96 us
    another operation x1, other arithmetic, shards(): return (jnp.stack(updated_list), jnp.stack(gram_list))  6.93 us
    all_to_all x1, starting transfers between devices, shards(): lax.all_to_all(send_rows, 'ingest', split_axis=0, concat_axis=0, tiled=True)  6.79 us
  transfers between devices with their start and end apart: 5, of which 4 were waited for; matrix products, arithmetic and copies ran while one was open for 42% of the time, Pallas kernels for 0%

commit v1 on v0

--- a/solution.py
+++ b/solution.py
@@ -1,12 +1,289 @@
+import functools
+
 import jax
 import jax.numpy as jnp
 from jax import lax
+from jax.experimental import pallas as pl
+from jax.experimental.pallas import tpu as pltpu
 from jax.sharding import PartitionSpec as P
 
 K = 4096
 BLK = 128
 P_SIZE = 64
 KB = 32
+CHUNKS = 2
+MESH = pl.DeviceIdType.MESH
+VMEM_BYTES = 48 * 1024 * 1024
+
+
+def whole(ref, sem):
+    return pltpu.make_async_copy(ref, ref, sem)
+
+
+def exchange_kernel(
+    n, own, cap,
+    codes_ref, vec_ref, book_ref,
+    got_ref, table_ref, member_ref,
+    allc, picks, ret, send, tabv, memv,
+    code_send, code_recv, one_send, one_recv, two_send, two_recv, local_sem, out_sem,
+):
+    me = lax.axis_index("ingest")
+    book = lax.axis_index("codes")
+    other = 1 - book
+    rows, dim = vec_ref.shape
+    width = dim // CHUNKS
+    slots = n * cap
+    f32, bf16, i32 = jnp.float32, jnp.bfloat16, jnp.int32
+
+    barrier = pltpu.get_barrier_semaphore()
+
+    def greet(step, carry):
+        peer = lax.rem(me + step, n)
+        pl.semaphore_signal(barrier, inc=1, device_id=(peer, book), device_id_type=MESH)
+        pl.semaphore_signal(barrier, inc=1, device_id=(peer, other), device_id_type=MESH)
+        return carry
+
+    pl.semaphore_signal(barrier, inc=1, device_id=(me, other), device_id_type=MESH)
+    lax.fori_loop(1, n, greet, 0)
+    pl.semaphore_wait(barrier, 2 * n - 1)
+
+    def code_copy(step):
+        peer = lax.rem(me + step, n)
+        return pltpu.make_async_remote_copy(
+            src_ref=codes_ref,
+            dst_ref=allc.at[me],
+            send_sem=code_send.at[step],
+            recv_sem=code_recv.at[me],
+            device_id=(peer, book),
+            device_id_type=MESH,
+        )
+
+    def start_codes(step, carry):
+        code_copy(step).start()
+        return carry
+
+    lax.fori_loop(1, n, start_codes, 0)
+
+    earlier = (
+        lax.broadcasted_iota(i32, (rows, rows), 0) < lax.broadcasted_iota(i32, (rows, rows), 1)
+    ).astype(bf16)
+    mine = codes_ref[...]
+    first, second = mine[0:1, :], mine[1:2, :]
+    own_code = jnp.where(book == 0, first, second)
+    oth_code = jnp.where(book == 0, second, first)
+
+    def slot_table(code):
+        target = code // own
+        hits = (target == lax.broadcasted_iota(i32, (n, rows), 0)).astype(f32)
+        before = jnp.dot(hits.astype(bf16), earlier, preferred_element_type=f32)
+        rank = jnp.sum(before * hits, axis=0, keepdims=True)
+        slot = target * cap + rank.astype(i32)
+        return (slot == lax.broadcasted_iota(i32, (slots, rows), 0)).astype(f32)
+
+    send_table = slot_table(own_code).astype(bf16)
+    merge_table = jnp.transpose(slot_table(oth_code)).astype(bf16)
+
+    allc[me] = mine
+
+    def wait_codes(step, carry):
+        source = lax.rem(me + step, n)
+        whole(allc.at[source], code_recv.at[source]).wait()
+        return carry
+
+    lax.fori_loop(1, n, wait_codes, 0)
+
+    all_codes = allc[...]
+    firsts, seconds = all_codes[:, 0, :], all_codes[:, 1, :]
+    own_all = jnp.where(book == 0, firsts, seconds)
+    oth_all = jnp.where(book == 0, seconds, firsts)
+    local = own_all - me * own
+    inside = (local >= 0) & (local < own)
+    before = jnp.dot(
+        jnp.where(inside, 1.0, 0.0).astype(bf16), earlier, preferred_element_type=f32
+    )
+    rank = jnp.where(inside, before, -1.0).astype(i32)
+    chosen = rank[:, None, :] == lax.broadcasted_iota(i32, (n, cap, rows), 1)
+    local_one = (local + 1).astype(f32)
+    oth_one = (oth_all + 1).astype(f32)
+    row_code = jnp.sum(jnp.where(chosen, local_one[:, None, :], 0.0), axis=2, keepdims=True)
+    oth_slot = jnp.sum(jnp.where(chosen, oth_one[:, None, :], 0.0), axis=2, keepdims=True)
+    row_code = row_code.reshape(slots, 1).astype(i32) - 1
+    oth_slot = oth_slot.reshape(slots, 1).astype(i32) - 1
+    member32 = (row_code == lax.broadcasted_iota(i32, (slots, own), 1)).astype(f32)
+    member = member32.astype(bf16)
+
+    for c in range(CHUNKS):
+        part = jnp.dot(
+            member, book_ref[:, c * width : (c + 1) * width], preferred_element_type=f32
+        )
+        picks[c] = part.astype(bf16).reshape(n, cap, width)
+
+        def start_one(step, carry):
+            peer = lax.rem(me + step, n)
+            pltpu.make_async_remote_copy(
+                src_ref=picks.at[c, peer],
+                dst_ref=ret.at[c, me],
+                send_sem=one_send.at[c],
+                recv_sem=one_recv.at[c],
+                device_id=(peer, other),
+                device_id_type=MESH,
+            ).start()
+            return carry
+
+        lax.fori_loop(0, n, start_one, 0)
+
+    memv[...] = jnp.transpose(member32).astype(bf16)
+    group = 4
+
+    def count_pairs(q, carry):
+        columns = lax.broadcasted_iota(i32, (slots, group * BLK), 1) + q * (group * BLK)
+        onehot = (oth_slot == columns).astype(f32).astype(bf16)
+        counts = jnp.dot(memv[...], onehot, preferred_element_type=f32)
+        for i in range(group):
+            tabv[q * group + i] = counts[:, i * BLK : (i + 1) * BLK]
+        return carry
+
+    lax.fori_loop(0, KB // group, count_pairs, 0)
+    table_copy = pltpu.make_async_copy(tabv, table_ref, out_sem.at[0])
+    table_copy.start()
+    member_copy = pltpu.make_async_copy(memv, member_ref, out_sem.at[1])
+    member_copy.start()
+
+    for c in range(CHUNKS):
+        whole(ret.at[c], one_recv.at[c]).wait()
+        rows_in = ret[c].reshape(slots, width)
+        fetched = jnp.dot(merge_table, rows_in, preferred_element_type=f32)
+        target = vec_ref[:, c * width : (c + 1) * width].astype(f32) - fetched
+        part = jnp.dot(send_table, target.astype(bf16), preferred_element_type=f32)
+        send[c] = part.astype(bf16).reshape(n, cap, width)
+
+        def start_two(step, carry):
+            peer = lax.rem(me + step, n)
+            pltpu.make_async_remote_copy(
+                src_ref=send.at[c, peer],
+                dst_ref=got_ref.at[c, me],
+                send_sem=two_send.at[c],
+                recv_sem=two_recv.at[c],
+                device_id=(peer, book),
+                device_id_type=MESH,
+            ).start()
+            return carry
+
+        lax.fori_loop(1, n, start_two, 0)
+        pltpu.make_async_copy(send.at[c, me], got_ref.at[c, me], local_sem.at[c]).start()
+
+    def wait_code_sends(step, carry):
+        code_copy(step).wait_send()
+        return carry
+
+    lax.fori_loop(1, n, wait_code_sends, 0)
+    table_copy.wait()
+    member_copy.wait()
+    for c in range(CHUNKS):
+        whole(picks.at[c], one_send.at[c]).wait()
+        whole(send.at[c, pl.ds(0, n - 1)], two_send.at[c]).wait()
+        pltpu.make_async_copy(send.at[c, me], got_ref.at[c, me], local_sem.at[c]).wait()
+        whole(got_ref.at[c, pl.ds(0, n - 1)], two_recv.at[c]).wait()
+
+
+def finish_kernel(
+    pieces, pairs_ref, got_ref, member_ref, table_ref, new_ref, gram_ref, tabv, newv, sems
+):
+    me = lax.axis_index("ingest")
+    book = lax.axis_index("codes")
+    first_row = book * KB + me * pieces
+    other_start = (1 - book) * KB
+    load = pltpu.make_async_copy(table_ref, tabv, sems.at[0])
+    load.start()
+    f32 = jnp.float32
+    member = member_ref[...]
+    load.wait()
+
+    for piece in range(pieces):
+
+        def place(p, carry):
+            block = pairs_ref[first_row + piece, p] - other_start
+            pltpu.make_async_copy(
+                tabv.at[block, pl.ds(piece * BLK, BLK)],
+                gram_ref.at[0, pl.ds(piece * BLK, BLK), pl.ds(pl.multiple_of(p * BLK, BLK), BLK)],
+                sems.at[1],
+            ).start()
+            return carry
+
+        lax.fori_loop(0, P_SIZE, place, 0)
+
+    count = jnp.sum(member.astype(f32), axis=1, keepdims=True)
+    scale = 1.0 / (count + 2.0)
+    slots = member.shape[1]
+    width = got_ref.shape[-1]
+    for c in range(CHUNKS):
+        rows_in = got_ref[c].reshape(slots, width)
+        total = jnp.dot(member, rows_in, preferred_element_type=f32)
+        newv[0, :, c * width : (c + 1) * width] = total * scale
+    store = pltpu.make_async_copy(newv, new_ref, sems.at[0])
+    store.start()
+    store.wait()
+    whole(gram_ref, sems.at[1]).wait()
+
+
+def two_books(vectors, codes, codebook, pairs):
+    n = lax.axis_size("ingest")
+    rows, dim = vectors.shape
+    own = codebook.shape[1]
+    cap = 2 * rows // n
+    slots = n * cap
+    width = dim // CHUNKS
+    f32, bf16 = jnp.float32, jnp.bfloat16
+    vmem = pl.BlockSpec(memory_space=pltpu.VMEM)
+    anywhere = pl.BlockSpec(memory_space=pl.ANY)
+    dma = pltpu.SemaphoreType.DMA
+    block = (CHUNKS, n, cap, width)
+    got, table, member = pl.pallas_call(
+        functools.partial(exchange_kernel, n, own, cap),
+        out_shape=(
+            jax.ShapeDtypeStruct(block, bf16),
+            jax.ShapeDtypeStruct((KB, own, BLK), f32),
+            jax.ShapeDtypeStruct((own, slots), bf16),
+        ),
+        in_specs=[vmem] * 3,
+        out_specs=(anywhere,) * 3,
+        scratch_shapes=[
+            pltpu.VMEM((n,) + codes.shape, jnp.int32),
+            pltpu.VMEM(block, bf16),
+            pltpu.VMEM(block, bf16),
+            pltpu.VMEM(block, bf16),
+            pltpu.VMEM((KB, own, BLK), f32),
+            pltpu.VMEM((own, slots), bf16),
+            dma((n,)),
+            dma((n,)),
+            dma((CHUNKS,)),
+            dma((CHUNKS,)),
+            dma((CHUNKS,)),
+            dma((CHUNKS,)),
+            dma((CHUNKS,)),
+            dma((2,)),
+        ],
+        compiler_params=pltpu.CompilerParams(
+            collective_id=0, has_side_effects=True, vmem_limit_bytes=VMEM_BYTES
+        ),
+        name="exchange",
+    )(codes, vectors, codebook[0])
+    return pl.pallas_call(
+        functools.partial(finish_kernel, own // BLK),
+        out_shape=(
+            jax.ShapeDtypeStruct((1, own, dim), f32),
+            jax.ShapeDtypeStruct((1, own, P_SIZE * BLK), f32),
+        ),
+        in_specs=[pl.BlockSpec(memory_space=pltpu.SMEM), vmem, vmem, anywhere],
+        out_specs=(anywhere, anywhere),
+        scratch_shapes=[
+            pltpu.VMEM((KB, own, BLK), f32),
+            pltpu.VMEM((1, own, dim), f32),
+            dma((2,)),
+        ],
+        compiler_params=pltpu.CompilerParams(vmem_limit_bytes=VMEM_BYTES),
+        name="finish",
+    )(pairs, got, member, table)
 
 
 def shards(vectors, codes, codebook, pairs):
@@ -105,4 +382,5 @@
 def solution(mesh):
     in_specs = (P("ingest", None), P(None, "ingest"), P("codes", "ingest", None), P())
     out_specs = (P("codes", "ingest", None), P("codes", "ingest", None))
-    return jax.shard_map(shards, mesh=mesh, in_specs=in_specs, out_specs=out_specs, check_vma=False)
+    part = two_books if mesh.shape["codes"] == 2 else shards
+    return jax.shard_map(part, mesh=mesh, in_specs=in_specs, out_specs=out_specs, check_vma=False)

time: 147 us -> 67.7 us (0.46)
  Pallas kernels: 0 us -> 60.8 us
  waiting for transfers between devices: 32.8 us -> 0 us
  matrix products: 26.3 us -> 0 us
  starting transfers between devices: 25.7 us -> 0 us
  local copies, waits for them, and re-layouts: 30.6 us -> 5.7 us
  other arithmetic: 16.7 us -> 0 us
  between operations: 14.5 us -> 0.66 us
    pallas_call x0 -> x2, Pallas kernels: none -> 60.8 us  [the longest x1 55.8 us: two_books(): pl.pallas_call(functools.partial(exchange_kernel, n, own, cap), out_shape...]
    dot_general x17 -> x0, matrix products: 26.3 us -> none  [the longest x16 24.7 us: shards(): lax.dot_general(member_part, onehot_table, contract, preferred_element_ty...]
    all_to_all x4 -> x0, starting transfers between devices: 25.4 us -> none  [the longest x1 8.31 us: shards(): lax.all_to_all(slot_request, 'ingest', split_axis=0, concat_axis=0, tiled...]
    psum x1 -> x0, waiting for transfers between devices: 17.3 us -> none  [shards(): lax.psum(partial_sum.astype(jnp.bfloat16), 'codes').astype(jnp.float32)]
    all_to_all x4 -> x0, waiting for transfers between devices: 15.5 us -> none  [the longest x1 11.3 us: shards(): lax.all_to_all(send_rows, 'ingest', split_axis=0, concat_axis=0, tiled=True)]
    eq x17 -> x0, local copies, waits for them, and re-layouts: 10.5 us -> none  [shards(): chosen[:, :, None] == jnp.arange(BLK, dtype=jnp.int32)]
    gather x7 -> x0, local copies, waits for them, and re-layouts: 8.06 us -> none  [the longest x1 2.06 us: shards(): jnp.take(flat_book, jnp.maximum(lax.all_to_all(slot_request, 'ingest', sp...]
    another operation x3 -> x0, other arithmetic: 7.56 us -> none  [the longest x1 6.93 us: shards(): return (jnp.stack(updated_list), jnp.stack(gram_list))]
  transfers between devices with their start and end apart: 5 -> 0, of which waited for: 4 -> 0; matrix products, arithmetic and copies ran while one was open for 42% -> 0% of each run, Pallas kernels for 0% -> 0%
where the time goes in v1:
time: 67.7 us; the launch traced here: 67.1 us
  Pallas kernels  60.8 us (90%)
  local copies, waits for them, and re-layouts  5.7 us (8%)
    pallas_call x1, Pallas kernels, two_books(): pl.pallas_call(functools.partial(exchange_kernel, n, own, cap), out_shape...  55.8 us
    unnamed x10, local copies, waits for them, and re-layouts  5.7 us
    pallas_call x1, Pallas kernels, two_books(): pl.pallas_call(functools.partial(finish_kernel, own // BLK), out_shape=(j...  4.96 us

profile of v1, /device:TPU:0, one launch (start us, length us, event | category | flops | bytes accessed | tf_op | source)
XLA Modules:
  0.0 67.1 jit_solution(12447320843211005865)
XLA Ops:
  0.6 0.0 copy-start.1
  0.6 1.0 %copy-done.1 = bf16[256,1024]{1,0:T(8,128)(2,1)S(1)} copy-done((bf16[256,1024]{1,0:T(8,128)(2,1)S(1)}, bf16[256,1024]{1,0:T(8,128)(2,1)}, u32[]{:S(2)}) %copy-start.1) | copy-done | bytes 524312
  1.7 0.0 copy-start.2
  1.7 1.0 %copy-done.2 = bf16[1,256,1024]{2,1,0:T(8,128)(2,1)S(1)} copy-done((bf16[1,256,1024]{2,1,0:T(8,128)(2,1)S(1)}, bf16[1,256,1024]{2,1,0:T(8,128)(2,1)}, u32[]{:S(2)}) %copy-start.2) | copy-done | bytes 524312
  2.7 0.0 copy-start.4
  2.7 0.7 %copy-done.4 = s32[2,256]{1,0:T(2,128)S(1)} copy-done((s32[2,256]{1,0:T(2,128)S(1)}, s32[2,256]{1,0:T(2,128)}, u32[]{:S(2)}) %copy-start.4) | copy-done | bytes 2072
  3.4 55.8 %exchange.1 = (bf16[2,16,32,512]{3,2,1,0:T(8,128)(2,1)S(1)}, f32[32,256,128]{2,1,0:T(8,128)}, bf16[256,512]{1,0:T(8,128)(2,1)S(1)}) custom-call(s32[2,256]{1,0:T(2,128)S(1)} %copy-done.4, bf16[256,1024]{1,0:T(8,128)(2,1)S(1)} %copy-done.1, bf16[256,1024]{1,0:T(8,128)(2,1)S(1)} %bitcast.1), custom_call_target="tpu_custom_call" | custom-call | tf_op jit(solution)/shard_map/exchange/pallas_call | solution.py:241
  59.2 0.0 copy-start
  59.2 2.2 %copy-done = f32[32,256,128]{2,1,0:T(8,128)S(1)} copy-done((f32[32,256,128]{2,1,0:T(8,128)S(1)}, f32[32,256,128]{2,1,0:T(8,128)}, u32[]{:S(2)}) %copy-start) | copy-done | bytes 4194328
  61.4 0.0 copy-start.3
  61.4 0.8 %copy-done.3 = s32[64,64]{1,0:T(8,128)S(1)} copy-done((s32[64,64]{1,0:T(8,128)S(1)}, s32[64,64]{1,0:T(8,128)}, u32[]{:S(2)}) %copy-start.3) | copy-done | bytes 16408
  62.2 5.0 %finish.1 = (f32[1,256,1024]{2,1,0:T(8,128)}, f32[1,256,8192]{2,1,0:T(8,128)}) custom-call(s32[64,64]{1,0:T(8,128)S(1)} %copy-done.3, bf16[2,16,32,512]{3,2,1,0:T(8,128)(2,1)S(1)} %get-tuple-element.5.got_ref, bf16[256,512]{1,0:T(8,128)(2,1)S(1)} %get-tuple-element.6.member_ref, f32[32,256,128]{2,1,0:T(8,128)S(1)} %copy-done), custom_call_target="tpu_custom_call" | custom-call | tf_op jit(solution)/shard_map/finish/pallas_call | solution.py:271
Async XLA Ops:
  0.6 1.0 %copy-start.1 = (bf16[256,1024]{1,0:T(8,128)(2,1)S(1)}, bf16[256,1024]{1,0:T(8,128)(2,1)}, u32[]{:S(2)}) copy-start(bf16[256,1024]{1,0:T(8,128)(2,1)} %vec_ref.1) | copy-start | bytes 1572868
  1.7 1.0 %copy-start.2 = (bf16[1,256,1024]{2,1,0:T(8,128)(2,1)S(1)}, bf16[1,256,1024]{2,1,0:T(8,128)(2,1)}, u32[]{:S(2)}) copy-start(bf16[1,256,1024]{2,1,0:T(8,128)(2,1)} %param.6) | copy-start | bytes 1572868
  2.7 0.7 %copy-start.4 = (s32[2,256]{1,0:T(2,128)S(1)}, s32[2,256]{1,0:T(2,128)}, u32[]{:S(2)}) copy-start(s32[2,256]{1,0:T(2,128)} %codes_ref.1) | copy-start | bytes 6148
  59.2 2.2 %copy-start = (f32[32,256,128]{2,1,0:T(8,128)S(1)}, f32[32,256,128]{2,1,0:T(8,128)}, u32[]{:S(2)}) copy-start(f32[32,256,128]{2,1,0:T(8,128)} %get-tuple-element.7.table_ref) | copy-start | bytes 12582916
  61.4 0.8 %copy-start.3 = (s32[64,64]{1,0:T(8,128)S(1)}, s32[64,64]{1,0:T(8,128)}, u32[]{:S(2)}) copy-start(s32[64,64]{1,0:T(8,128)} %pairs_ref.1) | copy-start | bytes 49156

commit v2 on v1

--- a/solution.py
+++ b/solution.py
@@ -13,7 +13,7 @@
 KB = 32
 CHUNKS = 2
 MESH = pl.DeviceIdType.MESH
-VMEM_BYTES = 48 * 1024 * 1024
+VMEM_BYTES = 32 * 1024 * 1024
 
 
 def whole(ref, sem):
@@ -22,10 +22,10 @@
 
 def exchange_kernel(
     n, own, cap,
-    codes_ref, vec_ref, book_ref,
-    got_ref, table_ref, member_ref,
-    allc, picks, ret, send, tabv, memv,
-    code_send, code_recv, one_send, one_recv, two_send, two_recv, local_sem, out_sem,
+    codes_hbm, vec_hbm, book_hbm, pairs_hbm,
+    got_ref, table_ref, member_ref, pairs_out,
+    codes_ref, vec_ref, book_ref, allc, picks, ret, send,
+    code_send, code_recv, one_send, one_recv, two_send, two_recv, local_sem, in_sem,
 ):
     me = lax.axis_index("ingest")
     book = lax.axis_index("codes")
@@ -35,6 +35,15 @@
     slots = n * cap
     f32, bf16, i32 = jnp.float32, jnp.bfloat16, jnp.int32
 
+    load_codes = pltpu.make_async_copy(codes_hbm, codes_ref, in_sem.at[0])
+    load_codes.start()
+    load_book = pltpu.make_async_copy(book_hbm, book_ref, in_sem.at[1])
+    load_book.start()
+    load_vectors = pltpu.make_async_copy(vec_hbm, vec_ref, in_sem.at[2])
+    load_vectors.start()
+    load_pairs = pltpu.make_async_copy(pairs_hbm, pairs_out, in_sem.at[3])
+    load_pairs.start()
+
     barrier = pltpu.get_barrier_semaphore()
 
     def greet(step, carry):
@@ -45,6 +54,7 @@
 
     pl.semaphore_signal(barrier, inc=1, device_id=(me, other), device_id_type=MESH)
     lax.fori_loop(1, n, greet, 0)
+    load_codes.wait()
     pl.semaphore_wait(barrier, 2 * n - 1)
 
     def code_copy(step):
@@ -104,13 +114,12 @@
     rank = jnp.where(inside, before, -1.0).astype(i32)
     chosen = rank[:, None, :] == lax.broadcasted_iota(i32, (n, cap, rows), 1)
     local_one = (local + 1).astype(f32)
-    oth_one = (oth_all + 1).astype(f32)
     row_code = jnp.sum(jnp.where(chosen, local_one[:, None, :], 0.0), axis=2, keepdims=True)
-    oth_slot = jnp.sum(jnp.where(chosen, oth_one[:, None, :], 0.0), axis=2, keepdims=True)
     row_code = row_code.reshape(slots, 1).astype(i32) - 1
-    oth_slot = oth_slot.reshape(slots, 1).astype(i32) - 1
     member32 = (row_code == lax.broadcasted_iota(i32, (slots, own), 1)).astype(f32)
     member = member32.astype(bf16)
+
+    load_book.wait()
 
     for c in range(CHUNKS):
         part = jnp.dot(
@@ -132,22 +141,23 @@
 
         lax.fori_loop(0, n, start_one, 0)
 
-    memv[...] = jnp.transpose(member32).astype(bf16)
+    oth_one = (oth_all + 1).astype(f32)
+    oth_slot = jnp.sum(jnp.where(chosen, oth_one[:, None, :], 0.0), axis=2, keepdims=True)
+    oth_slot = oth_slot.reshape(slots, 1).astype(i32) - 1
+    member_ref[...] = jnp.transpose(member32).astype(bf16)
     group = 4
 
     def count_pairs(q, carry):
         columns = lax.broadcasted_iota(i32, (slots, group * BLK), 1) + q * (group * BLK)
         onehot = (oth_slot == columns).astype(f32).astype(bf16)
-        counts = jnp.dot(memv[...], onehot, preferred_element_type=f32)
+        counts = jnp.dot(member_ref[...], onehot, preferred_element_type=f32)
         for i in range(group):
-            tabv[q * group + i] = counts[:, i * BLK : (i + 1) * BLK]
+            table_ref[q * group + i] = counts[:, i * BLK : (i + 1) * BLK]
         return carry
 
     lax.fori_loop(0, KB // group, count_pairs, 0)
-    table_copy = pltpu.make_async_copy(tabv, table_ref, out_sem.at[0])
-    table_copy.start()
-    member_copy = pltpu.make_async_copy(memv, member_ref, out_sem.at[1])
-    member_copy.start()
+    load_vectors.wait()
+    load_pairs.wait()
 
     for c in range(CHUNKS):
         whole(ret.at[c], one_recv.at[c]).wait()
@@ -177,8 +187,6 @@
         return carry
 
     lax.fori_loop(1, n, wait_code_sends, 0)
-    table_copy.wait()
-    member_copy.wait()
     for c in range(CHUNKS):
         whole(picks.at[c], one_send.at[c]).wait()
         whole(send.at[c, pl.ds(0, n - 1)], two_send.at[c]).wait()
@@ -187,13 +195,13 @@
 
 
 def finish_kernel(
-    pieces, pairs_ref, got_ref, member_ref, table_ref, new_ref, gram_ref, tabv, newv, sems
+    pieces, pairs_in, got_ref, member_ref, table_ref, new_ref, gram_ref, pairs_ref, newv, sems
 ):
     me = lax.axis_index("ingest")
     book = lax.axis_index("codes")
     first_row = book * KB + me * pieces
     other_start = (1 - book) * KB
-    load = pltpu.make_async_copy(table_ref, tabv, sems.at[0])
+    load = pltpu.make_async_copy(pairs_in, pairs_ref, sems.at[0])
     load.start()
     f32 = jnp.float32
     member = member_ref[...]
@@ -204,7 +212,7 @@
         def place(p, carry):
             block = pairs_ref[first_row + piece, p] - other_start
             pltpu.make_async_copy(
-                tabv.at[block, pl.ds(piece * BLK, BLK)],
+                table_ref.at[block, pl.ds(piece * BLK, BLK)],
                 gram_ref.at[0, pl.ds(piece * BLK, BLK), pl.ds(pl.multiple_of(p * BLK, BLK), BLK)],
                 sems.at[1],
             ).start()
@@ -235,25 +243,27 @@
     width = dim // CHUNKS
     f32, bf16 = jnp.float32, jnp.bfloat16
     vmem = pl.BlockSpec(memory_space=pltpu.VMEM)
-    anywhere = pl.BlockSpec(memory_space=pl.ANY)
+    hbm = pl.BlockSpec(memory_space=pltpu.HBM)
     dma = pltpu.SemaphoreType.DMA
     block = (CHUNKS, n, cap, width)
-    got, table, member = pl.pallas_call(
+    got, table, member, pairs = pl.pallas_call(
         functools.partial(exchange_kernel, n, own, cap),
         out_shape=(
             jax.ShapeDtypeStruct(block, bf16),
             jax.ShapeDtypeStruct((KB, own, BLK), f32),
             jax.ShapeDtypeStruct((own, slots), bf16),
+            jax.ShapeDtypeStruct(pairs.shape, jnp.int32),
         ),
-        in_specs=[vmem] * 3,
-        out_specs=(anywhere,) * 3,
+        in_specs=[hbm] * 4,
+        out_specs=(vmem,) * 4,
         scratch_shapes=[
+            pltpu.VMEM(codes.shape, jnp.int32),
+            pltpu.VMEM((rows, dim), bf16),
+            pltpu.VMEM((own, dim), bf16),
             pltpu.VMEM((n,) + codes.shape, jnp.int32),
             pltpu.VMEM(block, bf16),
             pltpu.VMEM(block, bf16),
             pltpu.VMEM(block, bf16),
-            pltpu.VMEM((KB, own, BLK), f32),
-            pltpu.VMEM((own, slots), bf16),
             dma((n,)),
             dma((n,)),
             dma((CHUNKS,)),
@@ -261,27 +271,27 @@
             dma((CHUNKS,)),
             dma((CHUNKS,)),
             dma((CHUNKS,)),
-            dma((2,)),
+            dma((4,)),
         ],
         compiler_params=pltpu.CompilerParams(
             collective_id=0, has_side_effects=True, vmem_limit_bytes=VMEM_BYTES
         ),
         name="exchange",
-    )(codes, vectors, codebook[0])
+    )(*(pltpu.with_memory_space_constraint(a, pltpu.HBM) for a in (codes, vectors, codebook[0], pairs)))
     return pl.pallas_call(
         functools.partial(finish_kernel, own // BLK),
         out_shape=(
             jax.ShapeDtypeStruct((1, own, dim), f32),
             jax.ShapeDtypeStruct((1, own, P_SIZE * BLK), f32),
         ),
-        in_specs=[pl.BlockSpec(memory_space=pltpu.SMEM), vmem, vmem, anywhere],
-        out_specs=(anywhere, anywhere),
+        in_specs=[vmem] * 4,
+        out_specs=(hbm, hbm),
         scratch_shapes=[
-            pltpu.VMEM((KB, own, BLK), f32),
+            pltpu.SMEM(pairs.shape, jnp.int32),
             pltpu.VMEM((1, own, dim), f32),
             dma((2,)),
         ],
-        compiler_params=pltpu.CompilerParams(vmem_limit_bytes=VMEM_BYTES),
+        compiler_params=pltpu.CompilerParams(vmem_limit_bytes=16 * 1024 * 1024),
         name="finish",
     )(pairs, got, member, table)
 

time: 67.7 us -> 61.6 us (0.910)
  local copies, waits for them, and re-layouts: 5.7 us -> 0 us
    unnamed x10 -> x0, local copies, waits for them, and re-layouts: 5.7 us -> none
where the time goes in v2:
time: 61.6 us; the launch traced here: 61.2 us
  Pallas kernels  60.5 us (98%)
  between operations  0.64 us (1%)
    pallas_call x1, Pallas kernels, two_books(): pl.pallas_call(functools.partial(exchange_kernel, n, own, cap), out_shape...  55.9 us
    pallas_call x1, Pallas kernels, two_books(): pl.pallas_call(functools.partial(finish_kernel, own // BLK), out_shape=(j...  4.66 us

profile of v2, /device:TPU:0, one launch (start us, length us, event | category | flops | bytes accessed | tf_op | source)
XLA Modules:
  0.0 61.2 jit_solution(9955510138129401378)
XLA Ops:
  0.6 55.9 %exchange.1 = (bf16[2,16,32,512]{3,2,1,0:T(8,128)(2,1)S(1)}, f32[32,256,128]{2,1,0:T(8,128)S(1)}, bf16[256,512]{1,0:T(8,128)(2,1)S(1)}, s32[64,64]{1,0:T(8,128)S(1)}) custom-call(s32[2,256]{1,0:T(2,128)} %codes_hbm.1, bf16[256,1024]{1,0:T(8,128)(2,1)} %vec_hbm.1, bf16[256,1024]{1,0:T(8,128)(2,1)} %bitcast.1, s32[64,64]{1,0:T(8,128)} %pairs_hbm.1), custom_call_target="tpu_custom_call" | custom-call | tf_op jit(solution)/shard_map/exchange/pallas_call | solution.py:249
  56.5 4.7 %finish.1 = (f32[1,256,1024]{2,1,0:T(8,128)}, f32[1,256,8192]{2,1,0:T(8,128)}) custom-call(s32[64,64]{1,0:T(8,128)S(1)} %get-tuple-element.6.pairs_in, bf16[2,16,32,512]{3,2,1,0:T(8,128)(2,1)S(1)} %get-tuple-element.7.got_ref, bf16[256,512]{1,0:T(8,128)(2,1)S(1)} %get-tuple-element.8.member_ref, f32[32,256,128]{2,1,0:T(8,128)S(1)} %get-tuple-element.9.table_ref), custom_call_target="tpu_custom_call" | custom-call | tf_op jit(solution)/shard_map/finish/pallas_call | solution.py:281

commit v3 on v2

--- a/solution.py
+++ b/solution.py
@@ -14,6 +14,34 @@
 CHUNKS = 2
 MESH = pl.DeviceIdType.MESH
 VMEM_BYTES = 32 * 1024 * 1024
+
+
+PLANE = 4
+
+
+def flipped(x, k):
+    low = x % 4
+    if k == 1:
+        return x + 1 - 2 * (low % 2)
+    if k == 2:
+        return x - low + (low + 2) % 4
+    if k == 3:
+        return x - low + 3 - low
+    return x
+
+
+def partners(me, n):
+    order = []
+    planes = n // PLANE
+    for base in range(0, planes, 4):
+        for k in (2, 3, 1, 0):
+            for j in range(PLANE):
+                if base or k or j:
+                    plane = me // PLANE
+                    peer = flipped(plane, k) if planes % 4 == 0 else plane
+                    peer = (peer + base) % planes
+                    order.append(peer * PLANE + flipped(me % PLANE, j))
+    return order
 
 
 def whole(ref, sem):
@@ -89,9 +117,6 @@
         rank = jnp.sum(before * hits, axis=0, keepdims=True)
         slot = target * cap + rank.astype(i32)
         return (slot == lax.broadcasted_iota(i32, (slots, rows), 0)).astype(f32)
-
-    send_table = slot_table(own_code).astype(bf16)
-    merge_table = jnp.transpose(slot_table(oth_code)).astype(bf16)
 
     allc[me] = mine
 
@@ -121,14 +146,14 @@
 
     load_book.wait()
 
-    for c in range(CHUNKS):
+    others = partners(me, n)
+
+    def start_one(c):
         part = jnp.dot(
             member, book_ref[:, c * width : (c + 1) * width], preferred_element_type=f32
         )
         picks[c] = part.astype(bf16).reshape(n, cap, width)
-
-        def start_one(step, carry):
-            peer = lax.rem(me + step, n)
+        for peer in others + [me]:
             pltpu.make_async_remote_copy(
                 src_ref=picks.at[c, peer],
                 dst_ref=ret.at[c, me],
@@ -137,9 +162,11 @@
                 device_id=(peer, other),
                 device_id_type=MESH,
             ).start()
-            return carry
-
-        lax.fori_loop(0, n, start_one, 0)
+
+    start_one(0)
+
+    send_table = slot_table(own_code).astype(bf16)
+    merge_table = jnp.transpose(slot_table(oth_code)).astype(bf16)
 
     oth_one = (oth_all + 1).astype(f32)
     oth_slot = jnp.sum(jnp.where(chosen, oth_one[:, None, :], 0.0), axis=2, keepdims=True)
@@ -156,6 +183,8 @@
         return carry
 
     lax.fori_loop(0, KB // group, count_pairs, 0)
+    for c in range(1, CHUNKS):
+        start_one(c)
     load_vectors.wait()
     load_pairs.wait()
 
@@ -167,8 +196,7 @@
         part = jnp.dot(send_table, target.astype(bf16), preferred_element_type=f32)
         send[c] = part.astype(bf16).reshape(n, cap, width)
 
-        def start_two(step, carry):
-            peer = lax.rem(me + step, n)
+        for peer in others:
             pltpu.make_async_remote_copy(
                 src_ref=send.at[c, peer],
                 dst_ref=got_ref.at[c, me],
@@ -177,9 +205,6 @@
                 device_id=(peer, book),
                 device_id_type=MESH,
             ).start()
-            return carry
-
-        lax.fori_loop(1, n, start_two, 0)
         pltpu.make_async_copy(send.at[c, me], got_ref.at[c, me], local_sem.at[c]).start()
 
     def wait_code_sends(step, carry):
@@ -392,5 +417,5 @@
 def solution(mesh):
     in_specs = (P("ingest", None), P(None, "ingest"), P("codes", "ingest", None), P())
     out_specs = (P("codes", "ingest", None), P("codes", "ingest", None))
-    part = two_books if mesh.shape["codes"] == 2 else shards
+    part = two_books if dict(mesh.shape) == {"ingest": 4 * PLANE, "codes": 2} else shards
     return jax.shard_map(part, mesh=mesh, in_specs=in_specs, out_specs=out_specs, check_vma=False)

time: 61.6 us -> 63.4 us (1.029)
  Pallas kernels: 60.5 us -> 62.6 us
    pallas_call x1, Pallas kernels: 55.9 us -> 58 us  [two_books(): pl.pallas_call(functools.partial(exchange_kernel, n, own, cap), out_shape...]
where the time goes in v3:
time: 63.4 us; the launch traced here: 63.3 us
  Pallas kernels  62.6 us (99%)
  between operations  0.64 us (1%)
    pallas_call x1, Pallas kernels, two_books(): pl.pallas_call(functools.partial(exchange_kernel, n, own, cap), out_shape...  58 us
    pallas_call x1, Pallas kernels, two_books(): pl.pallas_call(functools.partial(finish_kernel, own // BLK), out_shape=(j...  4.66 us

profile of v3, /device:TPU:0, one launch (start us, length us, event | category | flops | bytes accessed | tf_op | source)
XLA Modules:
  0.0 63.3 jit_solution(17881082280054779712)
XLA Ops:
  0.6 58.0 %exchange.1 = (bf16[2,16,32,512]{3,2,1,0:T(8,128)(2,1)S(1)}, f32[32,256,128]{2,1,0:T(8,128)S(1)}, bf16[256,512]{1,0:T(8,128)(2,1)S(1)}, s32[64,64]{1,0:T(8,128)S(1)}) custom-call(s32[2,256]{1,0:T(2,128)} %codes_hbm.1, bf16[256,1024]{1,0:T(8,128)(2,1)} %vec_hbm.1, bf16[256,1024]{1,0:T(8,128)(2,1)} %bitcast.1, s32[64,64]{1,0:T(8,128)} %pairs_hbm.1), custom_call_target="tpu_custom_call" | custom-call | tf_op jit(solution)/shard_map/exchange/pallas_call | solution.py:274
  58.6 4.7 %finish.1 = (f32[1,256,1024]{2,1,0:T(8,128)}, f32[1,256,8192]{2,1,0:T(8,128)}) custom-call(s32[64,64]{1,0:T(8,128)S(1)} %get-tuple-element.6.pairs_in, bf16[2,16,32,512]{3,2,1,0:T(8,128)(2,1)S(1)} %get-tuple-element.7.got_ref, bf16[256,512]{1,0:T(8,128)(2,1)S(1)} %get-tuple-element.8.member_ref, f32[32,256,128]{2,1,0:T(8,128)S(1)} %get-tuple-element.9.table_ref), custom_call_target="tpu_custom_call" | custom-call | tf_op jit(solution)/shard_map/finish/pallas_call | solution.py:306

commit v4 on v2

--- a/solution.py
+++ b/solution.py
@@ -141,21 +141,6 @@
 
         lax.fori_loop(0, n, start_one, 0)
 
-    oth_one = (oth_all + 1).astype(f32)
-    oth_slot = jnp.sum(jnp.where(chosen, oth_one[:, None, :], 0.0), axis=2, keepdims=True)
-    oth_slot = oth_slot.reshape(slots, 1).astype(i32) - 1
-    member_ref[...] = jnp.transpose(member32).astype(bf16)
-    group = 4
-
-    def count_pairs(q, carry):
-        columns = lax.broadcasted_iota(i32, (slots, group * BLK), 1) + q * (group * BLK)
-        onehot = (oth_slot == columns).astype(f32).astype(bf16)
-        counts = jnp.dot(member_ref[...], onehot, preferred_element_type=f32)
-        for i in range(group):
-            table_ref[q * group + i] = counts[:, i * BLK : (i + 1) * BLK]
-        return carry
-
-    lax.fori_loop(0, KB // group, count_pairs, 0)
     load_vectors.wait()
     load_pairs.wait()
 
@@ -182,6 +167,21 @@
         lax.fori_loop(1, n, start_two, 0)
         pltpu.make_async_copy(send.at[c, me], got_ref.at[c, me], local_sem.at[c]).start()
 
+    oth_one = (oth_all + 1).astype(f32)
+    oth_slot = jnp.sum(jnp.where(chosen, oth_one[:, None, :], 0.0), axis=2, keepdims=True)
+    oth_slot = oth_slot.reshape(slots, 1).astype(i32) - 1
+    member_ref[...] = jnp.transpose(member32).astype(bf16)
+    group = 4
+
+    def count_pairs(q, carry):
+        columns = lax.broadcasted_iota(i32, (slots, group * BLK), 1) + q * (group * BLK)
+        onehot = (oth_slot == columns).astype(f32).astype(bf16)
+        counts = jnp.dot(member_ref[...], onehot, preferred_element_type=f32)
+        for i in range(group):
+            table_ref[q * group + i] = counts[:, i * BLK : (i + 1) * BLK]
+        return carry
+
+    lax.fori_loop(0, KB // group, count_pairs, 0)
     def wait_code_sends(step, carry):
         code_copy(step).wait_send()
         return carry

time: 61.6 us -> 61.6 us (level)
  no operation moved by 1% of the time
where the time goes in v4:
time: 61.6 us; the launch traced here: 61.2 us
  Pallas kernels  60.5 us (98%)
  between operations  0.64 us (1%)
    pallas_call x1, Pallas kernels, two_books(): pl.pallas_call(functools.partial(exchange_kernel, n, own, cap), out_shape...  55.9 us
    pallas_call x1, Pallas kernels, two_books(): pl.pallas_call(functools.partial(finish_kernel, own // BLK), out_shape=(j...  4.66 us

profile of v4, /device:TPU:0, one launch (start us, length us, event | category | flops | bytes accessed | tf_op | source)
XLA Modules:
  0.0 61.2 jit_solution(2415065297736231161)
XLA Ops:
  0.6 55.9 %exchange.1 = (bf16[2,16,32,512]{3,2,1,0:T(8,128)(2,1)S(1)}, f32[32,256,128]{2,1,0:T(8,128)S(1)}, bf16[256,512]{1,0:T(8,128)(2,1)S(1)}, s32[64,64]{1,0:T(8,128)S(1)}) custom-call(s32[2,256]{1,0:T(2,128)} %codes_hbm.1, bf16[256,1024]{1,0:T(8,128)(2,1)} %vec_hbm.1, bf16[256,1024]{1,0:T(8,128)(2,1)} %bitcast.1, s32[64,64]{1,0:T(8,128)} %pairs_hbm.1), custom_call_target="tpu_custom_call" | custom-call | tf_op jit(solution)/shard_map/exchange/pallas_call | solution.py:249
  56.5 4.7 %finish.1 = (f32[1,256,1024]{2,1,0:T(8,128)}, f32[1,256,8192]{2,1,0:T(8,128)}) custom-call(s32[64,64]{1,0:T(8,128)S(1)} %get-tuple-element.6.pairs_in, bf16[2,16,32,512]{3,2,1,0:T(8,128)(2,1)S(1)} %get-tuple-element.7.got_ref, bf16[256,512]{1,0:T(8,128)(2,1)S(1)} %get-tuple-element.8.member_ref, f32[32,256,128]{2,1,0:T(8,128)S(1)} %get-tuple-element.9.table_ref), custom_call_target="tpu_custom_call" | custom-call | tf_op jit(solution)/shard_map/finish/pallas_call | solution.py:281

commit v5 on v4

--- a/solution.py
+++ b/solution.py
@@ -12,6 +12,7 @@
 P_SIZE = 64
 KB = 32
 CHUNKS = 2
+STORES = 8
 MESH = pl.DeviceIdType.MESH
 VMEM_BYTES = 32 * 1024 * 1024
 
@@ -23,8 +24,8 @@
 def exchange_kernel(
     n, own, cap,
     codes_hbm, vec_hbm, book_hbm, pairs_hbm,
-    got_ref, table_ref, member_ref, pairs_out,
-    codes_ref, vec_ref, book_ref, allc, picks, ret, send,
+    got_ref, blocks_ref, member_ref,
+    codes_ref, vec_ref, book_ref, allc, picks, ret, send, table_ref, pairs_ref,
     code_send, code_recv, one_send, one_recv, two_send, two_recv, local_sem, in_sem,
 ):
     me = lax.axis_index("ingest")
@@ -41,7 +42,7 @@
     load_book.start()
     load_vectors = pltpu.make_async_copy(vec_hbm, vec_ref, in_sem.at[2])
     load_vectors.start()
-    load_pairs = pltpu.make_async_copy(pairs_hbm, pairs_out, in_sem.at[3])
+    load_pairs = pltpu.make_async_copy(pairs_hbm, pairs_ref, in_sem.at[3])
     load_pairs.start()
 
     barrier = pltpu.get_barrier_semaphore()
@@ -182,6 +183,19 @@
         return carry
 
     lax.fori_loop(0, KB // group, count_pairs, 0)
+
+    pieces = own // BLK
+    for piece in range(pieces):
+        piece_rows = pl.ds(piece * BLK, BLK)
+
+        def put(p, carry):
+            block = pairs_ref[book * KB + me * pieces + piece, p] % KB
+            columns = pl.ds(pl.multiple_of(p * BLK, BLK), BLK)
+            blocks_ref[piece_rows, columns] = table_ref[block, piece_rows]
+            return carry
+
+        lax.fori_loop(0, P_SIZE, put, 0)
+
     def wait_code_sends(step, carry):
         code_copy(step).wait_send()
         return carry
@@ -194,32 +208,15 @@
         whole(got_ref.at[c, pl.ds(0, n - 1)], two_recv.at[c]).wait()
 
 
-def finish_kernel(
-    pieces, pairs_in, got_ref, member_ref, table_ref, new_ref, gram_ref, pairs_ref, newv, sems
-):
-    me = lax.axis_index("ingest")
-    book = lax.axis_index("codes")
-    first_row = book * KB + me * pieces
-    other_start = (1 - book) * KB
-    load = pltpu.make_async_copy(pairs_in, pairs_ref, sems.at[0])
-    load.start()
+def finish_kernel(got_ref, member_ref, blocks_ref, new_ref, gram_ref, newv, sems):
     f32 = jnp.float32
+    own = member_ref.shape[0]
+    for part in range(STORES):
+        part_rows = pl.ds(part * (own // STORES), own // STORES)
+        pltpu.make_async_copy(
+            blocks_ref.at[part_rows], gram_ref.at[0, part_rows], sems.at[1]
+        ).start()
     member = member_ref[...]
-    load.wait()
-
-    for piece in range(pieces):
-
-        def place(p, carry):
-            block = pairs_ref[first_row + piece, p] - other_start
-            pltpu.make_async_copy(
-                table_ref.at[block, pl.ds(piece * BLK, BLK)],
-                gram_ref.at[0, pl.ds(piece * BLK, BLK), pl.ds(pl.multiple_of(p * BLK, BLK), BLK)],
-                sems.at[1],
-            ).start()
-            return carry
-
-        lax.fori_loop(0, P_SIZE, place, 0)
-
     count = jnp.sum(member.astype(f32), axis=1, keepdims=True)
     scale = 1.0 / (count + 2.0)
     slots = member.shape[1]
@@ -231,7 +228,7 @@
     store = pltpu.make_async_copy(newv, new_ref, sems.at[0])
     store.start()
     store.wait()
-    whole(gram_ref, sems.at[1]).wait()
+    whole(blocks_ref, sems.at[1]).wait()
 
 
 def two_books(vectors, codes, codebook, pairs):
@@ -246,16 +243,15 @@
     hbm = pl.BlockSpec(memory_space=pltpu.HBM)
     dma = pltpu.SemaphoreType.DMA
     block = (CHUNKS, n, cap, width)
-    got, table, member, pairs = pl.pallas_call(
+    got, blocks, member = pl.pallas_call(
         functools.partial(exchange_kernel, n, own, cap),
         out_shape=(
             jax.ShapeDtypeStruct(block, bf16),
-            jax.ShapeDtypeStruct((KB, own, BLK), f32),
+            jax.ShapeDtypeStruct((own, P_SIZE * BLK), f32),
             jax.ShapeDtypeStruct((own, slots), bf16),
-            jax.ShapeDtypeStruct(pairs.shape, jnp.int32),
         ),
         in_specs=[hbm] * 4,
-        out_specs=(vmem,) * 4,
+        out_specs=(vmem,) * 3,
         scratch_shapes=[
             pltpu.VMEM(codes.shape, jnp.int32),
             pltpu.VMEM((rows, dim), bf16),
@@ -264,6 +260,8 @@
             pltpu.VMEM(block, bf16),
             pltpu.VMEM(block, bf16),
             pltpu.VMEM(block, bf16),
+            pltpu.VMEM((KB, own, BLK), f32),
+            pltpu.SMEM(pairs.shape, jnp.int32),
             dma((n,)),
             dma((n,)),
             dma((CHUNKS,)),
@@ -279,21 +277,20 @@
         name="exchange",
     )(*(pltpu.with_memory_space_constraint(a, pltpu.HBM) for a in (codes, vectors, codebook[0], pairs)))
     return pl.pallas_call(
-        functools.partial(finish_kernel, own // BLK),
+        finish_kernel,
         out_shape=(
             jax.ShapeDtypeStruct((1, own, dim), f32),
             jax.ShapeDtypeStruct((1, own, P_SIZE * BLK), f32),
         ),
-        in_specs=[vmem] * 4,
+        in_specs=[vmem] * 3,
         out_specs=(hbm, hbm),
         scratch_shapes=[
-            pltpu.SMEM(pairs.shape, jnp.int32),
             pltpu.VMEM((1, own, dim), f32),
             dma((2,)),
         ],
         compiler_params=pltpu.CompilerParams(vmem_limit_bytes=16 * 1024 * 1024),
         name="finish",
-    )(pairs, got, member, table)
+    )(got, member, blocks)
 
 
 def shards(vectors, codes, codebook, pairs):

time: 61.6 us -> 60.6 us (0.984)
  Pallas kernels: 60.5 us -> 59.5 us
    pallas_call x1, Pallas kernels: 4.66 us -> 3.65 us  [two_books(): pl.pallas_call(finish_kernel, out_shape=(jax.ShapeDtypeStruct((1, own, di...]
where the time goes in v5:
time: 60.6 us; the launch traced here: 60.1 us
  Pallas kernels  59.5 us (98%)
  between operations  0.64 us (1%)
    pallas_call x1, Pallas kernels, two_books(): pl.pallas_call(functools.partial(exchange_kernel, n, own, cap), out_shape...  55.9 us
    pallas_call x1, Pallas kernels, two_books(): pl.pallas_call(finish_kernel, out_shape=(jax.ShapeDtypeStruct((1, own, di...  3.65 us

profile of v5, /device:TPU:0, one launch (start us, length us, event | category | flops | bytes accessed | tf_op | source)
XLA Modules:
  0.0 60.1 jit_solution(2879116612183133010)
XLA Ops:
  0.6 55.9 %exchange.1 = (bf16[2,16,32,512]{3,2,1,0:T(8,128)(2,1)S(1)}, f32[256,8192]{1,0:T(8,128)S(1)}, bf16[256,512]{1,0:T(8,128)(2,1)S(1)}) custom-call(s32[2,256]{1,0:T(2,128)} %codes_hbm.1, bf16[256,1024]{1,0:T(8,128)(2,1)} %vec_hbm.1, bf16[256,1024]{1,0:T(8,128)(2,1)} %bitcast.1, s32[64,64]{1,0:T(8,128)} %pairs_hbm.1), custom_call_target="tpu_custom_call" | custom-call | tf_op jit(solution)/shard_map/exchange/pallas_call | solution.py:246
  56.5 3.6 %finish.1 = (f32[1,256,1024]{2,1,0:T(8,128)}, f32[1,256,8192]{2,1,0:T(8,128)}) custom-call(bf16[2,16,32,512]{3,2,1,0:T(8,128)(2,1)S(1)} %get-tuple-element.5.got_ref, bf16[256,512]{1,0:T(8,128)(2,1)S(1)} %get-tuple-element.6.member_ref, f32[256,8192]{1,0:T(8,128)S(1)} %get-tuple-element.7.blocks_ref), custom_call_target="tpu_custom_call" | custom-call | tf_op jit(solution)/shard_map/finish/pallas_call | solution.py:279
